TPU v7x, 256 devices: a whole 4x4x8 slice. The times are simulated.
256 devices in a mesh: ints: 16 (over x, y), amp: 16 (over z, core).
Axes of the slice: x: 4, y: 4, z: 8, core: 2. Of those that a mesh axis runs over, the one named last changes fastest.
Arguments:
- amplitudes: bfloat16 [1024, 32768], P('amp', 'ints'), may hold values from -6 to 6
- integrals: bfloat16 [32768, 16384], P('ints', 'amp'), may hold values from -0.125 to 0.125
- tile_map: int32 [16, 128], replicated, may hold values from 0 to 255, as said below
- residual_in: float32 [1024, 32768], P('amp', 'ints'), may hold values from -6 to 6
Outputs:
- residual: float32 [1024, 32768], P('amp', 'ints')
Inputs may be any that keep to these rules, and one draw needn't show every extreme that they name: `tile_map`: each row i names 128 different tiles, exactly 128 // 16 of them from each run of 16 consecutive tiles (t // 16 equal).
All inputs are finite; a program needn't handle non-finite values.
Results may differ from a plain program's by a relative error of at most 0.0003.
Values may be sent and summed in bfloat16 or wider, within the bound.
A program may use at most 64 MiB of HBM per device.

v0:
```python
import jax
import jax.numpy as jnp
from jax import lax
from jax.sharding import PartitionSpec as P

TILE = 128
TPD = 16
ABD = 8


def local(amplitudes, integrals, tile_map, residual_in):
    rows_dev = amplitudes.shape[0]
    amp_count = lax.axis_size("amp")
    ints_count = lax.axis_size("ints")
    partial_value = jnp.dot(
        lax.all_gather(amplitudes, "amp", axis=0, tiled=True),
        integrals,
        preferred_element_type=jnp.float32,
    )
    partial_value = partial_value.reshape(rows_dev * amp_count, ABD, TILE)
    received = lax.all_to_all(partial_value, "amp", split_axis=0, concat_axis=1, tiled=True)
    here = lax.axis_index("ints")
    tile_ids = lax.dynamic_index_in_dim(tile_map, here, 0, keepdims=False)
    dense_sums = jnp.zeros((rows_dev, ints_count * TPD, TILE), jnp.float32)
    dense_sums = dense_sums.at[:, tile_ids].add(received)
    summed = lax.psum_scatter(dense_sums, "ints", scatter_dimension=1, tiled=True)
    return residual_in + summed.reshape(rows_dev, TPD * TILE)


def solution(mesh):
    in_specs = (P("amp", "ints"), P("ints", "amp"), P(), P("amp", "ints"))
    out_specs = P("amp", "ints")
    return jax.shard_map(local, mesh=mesh, in_specs=in_specs, out_specs=out_specs, check_vma=False)
```

profile of v0, /device:TPU:32, one launch (start us, length us, event | category | flops | bytes accessed | tf_op | source)
XLA Modules:
  0.0 297.5 jit_solution(11454551511294370925)
XLA Ops:
  6.5 0.0 all-gather.2.cloned.1.call-start
  6.5 0.7 all-gather.2.cloned.1.call-update
  7.3 46.4 %all-gather.2.cloned.1.call-done = bf16[1024,2048]{1,0:T(8,128)(2,1)} async-done(((bf16[64,2048]{1,0:T(8,128)(2,1)}), bf16[1024,2048]{1,0:T(8,128)(2,1)}) %all-gather.2.cloned.1.call-update) | async-done | bytes 4194320 | tf_op jit(solution)/shard_map/all_gather | solution.py:16
  53.6 10.0 %fusion.1 = f32[1024,1024]{0,1:T(8,128)} fusion(bf16[1024,2048]{1,0:T(8,128)(2,1)} %all-gather.2.cloned.1.call-done, bf16[2048,1024]{1,0:T(8,128)(2,1)} %param.5), kind=kOutput, calls=%fused_computation.5 | convolution fusion | flops 4294967296 | bytes 12582912 | tf_op jit(solution)/shard_map/dot_general | solution.py:15
  63.6 5.4 %copy.8 = f32[1024,8,128]{2,1,0:T(8,128)} copy(f32[1024,8,128]{0,2,1:T(8,128)} %bitcast.21) | data formatting | bytes 8388608 | tf_op jit(solution)/shard_map/reshape | solution.py:20
  69.0 5.1 %all-to-all-start = ((f32[1024,8,128]{2,1,0:T(8,128)}), f32[1024,8,128]{2,1,0:T(8,128)}, u32[]{:S(2)}, u32[]{:S(2)}) async-start(f32[1024,8,128]{2,1,0:T(8,128)} %copy.8), calls=%async_computation | async-start | bytes 8388608 | tf_op jit(solution)/shard_map/all_to_all | solution.py:21
  74.1 0.0 reduce-scatter.2.cloned.1.call-start
  74.1 0.7 fusion
  74.8 91.7 %all-to-all-done = f32[1024,8,128]{2,1,0:T(8,128)} async-done(((f32[1024,8,128]{2,1,0:T(8,128)}), f32[1024,8,128]{2,1,0:T(8,128)}, u32[]{:S(2)}, u32[]{:S(2)}) %all-to-all-start) | async-done | bytes 4194336 | tf_op jit(solution)/shard_map/all_to_all | solution.py:21
  166.5 2.7 copy.15
  169.3 4.4 %copy.10 = f32[128,64,128]{2,1,0:T(8,128)} copy(f32[128,64,128]{2,0,1:T(8,128)S(1)} %bitcast.20) | data formatting | bytes 8388608 | tf_op jit(solution)/shard_map/all_to_all | solution.py:21
  173.6 4.3 %broadcast_in_dim.4 = f32[64,256,128]{2,0,1:T(8,128)} broadcast(f32[]{:T(128)} %constant.4.clone.1), dimensions={} | broadcast | bytes 8388612 | tf_op jit(solution)/shard_map/broadcast_in_dim | solution.py:24
  177.9 20.2 %scatter_fusion = f32[64,256,128]{2,0,1:T(8,128)} fusion(f32[64,256,128]{2,0,1:T(8,128)} %broadcast_in_dim.4, s32[128]{0:T(128)S(1)} %fusion, f32[128,64,128]{2,1,0:T(8,128)} %copy.10), kind=kCustom, calls=%fused_computation | custom fusion | flops 1048576 | bytes 12583424 | tf_op jit(solution)/shard_map/scatter-add | solution.py:25
  198.1 0.0 copy-start
  198.1 0.0 reduce-scatter.2.cloned.1.call-update
  198.1 90.7 %reduce-scatter.2.cloned.1.call-done = f32[64,16,128]{2,0,1:T(8,128)} async-done(((f32[64,256,128]{2,0,1:T(8,128)}), f32[64,16,128]{2,0,1:T(8,128)}) %reduce-scatter.2.cloned.1.call-update) | async-done | bytes 524304 | tf_op jit(solution)/shard_map/reduce_scatter | solution.py:26
  288.8 0.0 copy-done
  288.8 1.9 bitcast_add_fusion
Async XLA Ops:
  6.5 47.1 %all-gather.2.cloned.1.call-start = ((), (), s32[]{:S(2)}) async-start(), calls=%async_computation.2 | async-start | bytes 4456448 | tf_op jit(solution)/shard_map/all_gather | solution.py:16
  69.0 97.5 %all-to-all-start = ((f32[1024,8,128]{2,1,0:T(8,128)}), f32[1024,8,128]{2,1,0:T(8,128)}, u32[]{:S(2)}, u32[]{:S(2)}) async-start(f32[1024,8,128]{2,1,0:T(8,128)} %copy.8), calls=%async_computation | async-start | bytes 8388608 | tf_op jit(solution)/shard_map/all_to_all | solution.py:21
  74.1 214.7 %reduce-scatter.2.cloned.1.call-start = ((), (), s32[]{:S(2)}) async-start(), calls=%async_computation.3 | async-start | bytes 8912896 | tf_op jit(solution)/shard_map/reduce_scatter | solution.py:26
  198.1 90.7 %copy-start = (f32[64,2048]{1,0:T(8,128)S(1)}, f32[64,2048]{1,0:T(8,128)}, u32[]{:S(2)}) copy-start(f32[64,2048]{1,0:T(8,128)} %param.7) | copy-start | bytes 1572868
Sparse Core Ops, SparseCore 0:
  9.2 44.4 all-gather.1
  198.2 90.5 reduce-scatter.1
where the time goes:
time: 298 us
  waiting for transfers between devices  229 us (77%)
  other arithmetic  22.7 us (8%)
  local copies, waits for them, and re-layouts  16.8 us (6%)
  between operations  13.4 us (4%)
  matrix products  9.97 us (3%)
  starting transfers between devices  5.12 us (2%)
    all_to_all x1, waiting for transfers between devices, local(): lax.all_to_all(partial_value, 'amp', split_axis=0, concat_axis=1, tiled=T...  91.7 us
    reduce_scatter x1, waiting for transfers between devices, local(): lax.psum_scatter(dense_sums, 'ints', scatter_dimension=1, tiled=True)  90.7 us
    all_gather x1, waiting for transfers between devices, local(): lax.all_gather(amplitudes, 'amp', axis=0, tiled=True)  46.4 us
    scatter-add x1, other arithmetic, local(): dense_sums = dense_sums.at[:, tile_ids].add(received)  20.2 us
    dot_general x1, matrix products, local(): jnp.dot(lax.all_gather(amplitudes, 'amp', axis=0, tiled=True), integrals,...  9.97 us
    all_to_all x2, local copies, waits for them, and re-layouts, local(): lax.all_to_all(partial_value, 'amp', split_axis=0, concat_axis=1, tiled=T...  7.12 us
  transfers between devices with their start and end apart: 3, of which 3 were waited for; matrix products, arithmetic and copies ran while one was open for 0% of the time, Pallas kernels for 0%

commit v1 on v0

v1 whole, which is shorter than its diff:
```python
import math

import jax
import jax.numpy as jnp
from jax import lax
from jax.experimental import pallas as pl
from jax.experimental.pallas import tpu as pltpu
from jax.sharding import PartitionSpec as P

MESH = pl.DeviceIdType.MESH
F32, BF16, I16 = jnp.float32, jnp.bfloat16, jnp.int16

TOP = math.log2(1537.0)
SPAN = 24.0
STEPS = 32700.0 / SPAN
LOW = TOP - SPAN
XMIN = 2.0 ** LOW


def log_code(x):
    size = jnp.log2(jnp.maximum(jnp.abs(x), XMIN)) * STEPS + (0.5 - LOW * STEPS)
    return jnp.where(x < 0, -size, size)


def log_value(code):
    size = jnp.exp2(jnp.abs(code) * (1.0 / STEPS) + LOW)
    return jnp.where(code == 0, 0.0, jnp.where(code < 0, -size, size))


def chain_code(x):
    x = x.reshape(32, 8, 256)
    top = jnp.max(jnp.abs(x), axis=0)
    power = jnp.ceil(jnp.log2(jnp.maximum(top, 1e-30)) * 64.0)
    q = x * (jnp.exp2(power * (-1.0 / 64.0)) * 32700.0)[None]
    q = jnp.where(q < 0, q - 0.5, q + 0.5)
    return q.reshape(256, 256).astype(I16), jnp.concatenate([power, power], axis=0).astype(I16)


def chain_value(codes, powers):
    scale = jnp.exp2(powers.astype(F32)[0:8] * (1.0 / 64.0)) * (1.0 / 32700.0)
    return (codes.astype(F32).reshape(32, 8, 256) * scale[None]).reshape(256, 256)


def kernel(amp_ref, int_hbm, map_ref, out_ref,
           g, b, f, e, r13, r04, d, sb, rb, fs, fr, pick,
           ag_send, ag_recv, sib_send, sib_recv, loc_sem,
           xa_send, xa_recv, xa_loc, rs_send, rs_recv, fin_send, fin_recv, fin_loc):
    i = lax.axis_index("ints")
    a = lax.axis_index("amp")
    zz, c = a // 2, lax.rem(a, 2)
    x, y = i // 4, lax.rem(i, 4)
    me = i * 2 + c
    zr, zl = lax.rem(zz + 1, 8), lax.rem(zz + 7, 8)
    right, left, sib = (i, zr * 2 + c), (i, zl * 2 + c), (i, zz * 2 + 1 - c)
    lane0 = pl.multiple_of(c * 64, 64)

    def peer(t):
        dj = t // 2
        j = lax.rem(x + dj // 4, 4) * 4 + lax.rem(y + lax.rem(dj, 4), 4)
        return j, lax.rem(c + lax.rem(t, 2), 2)

    load_b = pltpu.make_async_copy(int_hbm, b, loc_sem.at[0])
    load_b.start()
    own = pltpu.make_async_copy(amp_ref, g.at[0, pl.ds(lane0, 64)], loc_sem.at[1])
    own.start()

    barrier = pltpu.get_barrier_semaphore()

    def greet(t, carry):
        j, cc = peer(t)
        pl.semaphore_signal(barrier, inc=1, device_id=(j, zz * 2 + cc), device_id_type=MESH)
        return carry
    for zn in (zr, zl):
        for cc in (0, 1):
            pl.semaphore_signal(barrier, inc=1, device_id=(i, zn * 2 + cc), device_id_type=MESH)
    lax.fori_loop(1, 32, greet, 0)

    lane = lax.broadcasted_iota(jnp.int32, (128, 256), 0)
    ent = lax.broadcasted_iota(jnp.int32, (128, 256), 1)
    spread = (lane == zz * 16 + lax.rem(ent, 16)).astype(F32).astype(BF16)
    rows = jnp.dot(map_ref[...].astype(F32).astype(BF16), spread, preferred_element_type=F32)
    blk = lax.broadcasted_iota(jnp.int32, (16, 256), 0)
    ent16 = lax.broadcasted_iota(jnp.int32, (16, 256), 1)
    ids = jnp.sum(jnp.where(blk == ent16 // 16, rows, 0.0), axis=0, keepdims=True)
    tiles = lax.broadcasted_iota(jnp.int32, (256, 256), 0).astype(F32)
    pick[...] = jnp.where(tiles == ids, 1.0, 0.0).astype(BF16)

    pl.semaphore_wait(barrier, 35)

    def part(ref, p):
        return ref.at[pl.ds(pl.multiple_of(lane0 + p * 32, 32), 32)]

    def slot(direction, k):
        return 0 if k == 0 else 7 if k == 4 else 2 * k - 1 + direction

    def hop(direction, k, p):
        src = amp_ref.at[pl.ds(p * 32, 32)] if k == 1 else part(g.at[slot(direction, k - 1)], p)
        return pltpu.make_async_remote_copy(
            src_ref=src, dst_ref=part(g.at[slot(direction, k)], p),
            send_sem=ag_send.at[direction, k - 1, p], recv_sem=ag_recv.at[direction, k - 1, p],
            device_id=(right, left)[direction], device_id_type=MESH)

    def share(direction, k, p):
        ref = part(g.at[slot(direction, k)], p)
        return pltpu.make_async_remote_copy(
            src_ref=ref, dst_ref=ref,
            send_sem=sib_send.at[direction, k - 1, p], recv_sem=sib_recv.at[direction, k - 1, p],
            device_id=sib, device_id_type=MESH)

    def pieces(direction, k):
        return (0, 1) if k < 4 else (direction,)

    for p in (0, 1):
        for direction in (0, 1):
            hop(direction, 1, p).start()
    share0 = pltpu.make_async_remote_copy(
        src_ref=amp_ref, dst_ref=g.at[0, pl.ds(lane0, 64)], send_sem=loc_sem.at[2], recv_sem=loc_sem.at[3],
        device_id=sib, device_id_type=MESH)
    share0.start()

    def pass_on(k):
        for p in (0, 1):
            for direction in (0, 1):
                if p in pieces(direction, k):
                    hop(direction, k, p).wait_recv()
                    if k < 4 and p in pieces(direction, k + 1):
                        hop(direction, k + 1, p).start()
                    share(direction, k, p).start()
        for p in (0, 1):
            for direction in (0, 1):
                if p in pieces(direction, k):
                    share(direction, k, p).wait_recv()

    def multiply(first, count):
        m = count * 128

        def columns(n, carry):
            left_side = g[pl.ds(first, count)].reshape(m, 2048)
            acc = jnp.dot(left_side, b[:, pl.ds(pl.multiple_of(n * 256, 256), 256)], preferred_element_type=F32)
            code = log_code(acc)
            for s in (0, 1):
                f[pl.ds(2 * n + s, m, stride=8), :] = code[:, s * 128:(s + 1) * 128]
            return carry
        lax.fori_loop(0, 4, columns, 0)

        def pack(q, carry):
            base = pl.multiple_of(q * 256, 256)
            even = f[pl.ds(base, 128), :].reshape(16, 8, 128)
            odd = f[pl.ds(base + 128, 128), :].reshape(16, 8, 128)
            e[first + q // 4, lax.rem(q // 2, 2), lax.rem(q, 2)] = jnp.concatenate([even, odd], axis=1).astype(I16)
            return carry
        lax.fori_loop(0, 4 * count, pack, 0)

    def deal_refs(k, j, cc):
        if k in (0, 4):
            return e.at[0 if k == 0 else 7, cc, :, j], r04.at[k // 4, me]
        return e.at[2 * k - cc, :, :, j], r13.at[k - 1, me]

    def deal(k):
        def one(t, carry):
            j, cc = peer(t)
            src, dst = deal_refs(k, j, cc)
            pltpu.make_async_remote_copy(
                src_ref=src, dst_ref=dst, send_sem=xa_send.at[k], recv_sem=xa_recv.at[k],
                device_id=(j, zz * 2 + cc), device_id_type=MESH).start()
            return carry
        src, dst = deal_refs(k, i, c)
        pltpu.make_async_copy(src, dst, xa_loc.at[k]).start()
        lax.fori_loop(1, 32, one, 0)

    def deal_all(k):
        ref = (r04.at[k // 4] if k in (0, 4) else r13.at[k - 1]).at[pl.ds(0, 31)]
        return pltpu.make_async_remote_copy(
            src_ref=ref, dst_ref=ref, send_sem=xa_send.at[k], recv_sem=xa_recv.at[k],
            device_id=sib, device_id_type=MESH)

    def gathered(k):
        src, dst = deal_refs(k, i, c)
        pltpu.make_async_copy(src, dst, xa_loc.at[k]).wait()
        deal_all(k).wait_recv()

    def add_up(codes, at):
        v = log_value(codes.astype(F32)).reshape(32, 2, 8, 128)
        v = jnp.concatenate([v[:, 0].reshape(256, 128), v[:, 1].reshape(256, 128)], axis=1)
        hi = v.astype(BF16)
        lo = (v - hi.astype(F32)).astype(BF16)
        d[at] = (jnp.dot(pick[...], hi, preferred_element_type=F32)
                 + jnp.dot(pick[...], lo, preferred_element_type=F32))

    def dense(k):
        gathered(k)
        if k in (0, 4):
            def one(q, carry):
                add_up(r04[k // 4, :, q], (12 if k == 0 else 14) + q)
                return carry
            lax.fori_loop(0, 2, one, 0)
        else:
            def one(q, carry):
                add_up(r13[k - 1, :, q // 2, lax.rem(q, 2)], (k - 1) * 4 + q)
                return carry
            lax.fori_loop(0, 4, one, 0)

    ahead = jnp.where(c == 0, zr, zl)

    def chain(k, lane, p):
        m = p if k == 4 else (10, 6, 2)[k - 1] + lane * 2 + p
        to = m if k > 1 else 10 + c * 2 + p
        return m, pltpu.make_async_remote_copy(
            src_ref=sb.at[m], dst_ref=rb.at[to], send_sem=rs_send.at[m], recv_sem=rs_recv.at[to],
            device_id=(i, ahead * 2 + (c if k > 1 else lane)), device_id_type=MESH)

    def arrived(m):
        pltpu.make_async_remote_copy(
            src_ref=rb.at[m], dst_ref=rb.at[m], send_sem=rs_send.at[m], recv_sem=rs_recv.at[m],
            device_id=sib, device_id_type=MESH).wait_recv()
        return chain_value(rb[m, 0:256], rb[m, 256:272])

    def send_chain(k, lane, p):
        own_at = 14 + p if k == 4 else (k - 1) * 4 + lane * 2 + p
        value = d[own_at]
        if k < 3:
            value = value + arrived((6, 2)[k - 1] + lane * 2 + p)
        m, copy = chain(k, lane, p)
        sb[m, 0:256], sb[m, 256:272] = chain_code(value)
        copy.start()

    def send_chain3(p):
        value = d[8 + c * 2 + p] + arrived(p)
        m, copy = chain(3, c, p)
        sb[m, 0:256], sb[m, 256:272] = chain_code(value)
        copy.start()

    own.wait()
    share0.wait_recv()
    load_b.wait()
    multiply(0, 1)
    deal(0)
    for k in (1, 2, 3):
        pass_on(k)
        multiply(2 * k - 1, 2)
        deal(k)
        dense(k - 1)
    pass_on(4)
    multiply(7, 1)
    deal(4)
    dense(3)

    def rest3(p, carry):
        send_chain(3, 1 - c, p)
        return carry
    lax.fori_loop(0, 2, rest3, 0)
    dense(4)

    def first4(p, carry):
        send_chain(4, c, p)
        return carry
    lax.fori_loop(0, 2, first4, 0)

    def own3(p, carry):
        send_chain3(p)
        return carry
    lax.fori_loop(0, 2, own3, 0)
    for k in (2, 1):
        def step(q, carry):
            lane = jnp.where(q < 2, 1 - c, c)
            send_chain(k, lane, lax.rem(q, 2))
            return carry
        lax.fori_loop(0, 4, step, 0)

    def last(p, j):
        return pltpu.make_async_remote_copy(
            src_ref=fs.at[p, :, pl.ds(pl.multiple_of(j * 16, 16), 16)],
            dst_ref=fr.at[p, :, pl.ds(pl.multiple_of(i * 16, 16), 16)],
            send_sem=fin_send.at[p], recv_sem=fin_recv.at[p], device_id=(j, zz * 2 + c), device_id_type=MESH)

    def keep(p):
        mine = pl.ds(pl.multiple_of(i * 16, 16), 16)
        return pltpu.make_async_copy(fs.at[p, :, mine], fr.at[p, :, mine], fin_loc.at[p])

    for p in (0, 1):
        total = d[12 + p] + arrived(10 + p) + arrived(12 + p)
        fs[p, 0] = total[:, 0:128]
        fs[p, 1] = total[:, 128:256]
        keep(p).start()

        def owners(t, carry):
            j, _ = peer(2 * t)
            last(p, j).start()
            return carry
        lax.fori_loop(1, 16, owners, 0)
    for p in (0, 1):
        keep(p).wait()
        every = fr.at[p, :, pl.ds(0, 240)]
        done = pltpu.make_async_remote_copy(
            src_ref=every, dst_ref=every, send_sem=fin_send.at[p], recv_sem=fin_recv.at[p],
            device_id=sib, device_id_type=MESH)
        done.wait_recv()
        for rr in (0, 1):
            for t in range(16):
                out_ref[p * 32 + rr * 16:p * 32 + rr * 16 + 16, t * 128:(t + 1) * 128] = (
                    fr[p, rr, pl.ds(t, 16, stride=16), :])
        done.wait_send()

    share0.wait_send()
    for k in (1, 2, 3, 4):
        for direction in (0, 1):
            for p in pieces(direction, k):
                hop(direction, k, p).wait_send()
                share(direction, k, p).wait_send()
    for k in range(5):
        deal_all(k).wait_send()
    for m in range(14):
        pltpu.make_async_remote_copy(
            src_ref=sb.at[m], dst_ref=rb.at[m], send_sem=rs_send.at[m], recv_sem=rs_recv.at[m],
            device_id=sib, device_id_type=MESH).wait_send()


def local(amplitudes, integrals, tile_map, residual_in):
    dma = pltpu.SemaphoreType.DMA
    ladder = pl.pallas_call(
        kernel,
        name="ladder",
        out_shape=jax.ShapeDtypeStruct((64, 2048), F32),
        in_specs=[pl.BlockSpec(memory_space=pltpu.VMEM), pl.BlockSpec(memory_space=pl.ANY),
                  pl.BlockSpec(memory_space=pltpu.VMEM)],
        out_specs=pl.BlockSpec(memory_space=pltpu.VMEM),
        scratch_shapes=[
            pltpu.VMEM((8, 128, 2048), BF16),
            pltpu.VMEM((2048, 1024), BF16),
            pltpu.VMEM((2048, 128), F32),
            pltpu.VMEM((8, 2, 2, 16, 16, 128), I16),
            pltpu.VMEM((3, 32, 2, 2, 16, 128), I16),
            pltpu.VMEM((2, 32, 2, 16, 128), I16),
            pltpu.VMEM((16, 256, 256), F32),
            pltpu.VMEM((14, 272, 256), I16),
            pltpu.VMEM((14, 272, 256), I16),
            pltpu.VMEM((2, 2, 256, 128), F32),
            pltpu.VMEM((2, 2, 256, 128), F32),
            pltpu.VMEM((256, 256), BF16),
            dma((2, 4, 2)), dma((2, 4, 2)), dma((2, 4, 2)), dma((2, 4, 2)), dma((4,)),
            dma((5,)), dma((5,)), dma((5,)), dma((14,)), dma((14,)), dma((2,)), dma((2,)), dma((2,)),
        ],
        compiler_params=pltpu.CompilerParams(
            collective_id=0, has_side_effects=True, vmem_limit_bytes=56 * 2**20),
    )(amplitudes, integrals, tile_map)
    return residual_in + ladder


def solution(mesh):
    in_specs = (P("amp", "ints"), P("ints", "amp"), P(), P("amp", "ints"))
    out_specs = P("amp", "ints")
    return jax.shard_map(local, mesh=mesh, in_specs=in_specs, out_specs=out_specs, check_vma=False)
```

time: 298 us -> 85.2 us (0.29)
  waiting for transfers between devices: 229 us -> 0 us
  Pallas kernels: 0 us -> 83.2 us
  other arithmetic: 22.7 us -> 1.89 us
  local copies, waits for them, and re-layouts: 16.8 us -> 0.01 us
  between operations: 13.4 us -> 0.02 us
  matrix products: 9.97 us -> 0 us
  starting transfers between devices: 5.12 us -> 0 us
    all_to_all x1 -> x0, waiting for transfers between devices: 91.7 us -> none  [local(): lax.all_to_all(partial_value, 'amp', split_axis=0, concat_axis=1, tiled=T...]
    reduce_scatter x1 -> x0, waiting for transfers between devices: 90.7 us -> none  [local(): lax.psum_scatter(dense_sums, 'ints', scatter_dimension=1, tiled=True)]
    pallas_call x0 -> x1, Pallas kernels: none -> 83.2 us  [local(): pl.pallas_call(kernel, name='ladder', out_shape=jax.ShapeDtypeStruct((64,...]
    all_gather x1 -> x0, waiting for transfers between devices: 46.4 us -> none  [local(): lax.all_gather(amplitudes, 'amp', axis=0, tiled=True)]
    scatter-add x1 -> x0, other arithmetic: 20.2 us -> none  [local(): dense_sums = dense_sums.at[:, tile_ids].add(received)]
    dot_general x1 -> x0, matrix products: 9.97 us -> none  [local(): jnp.dot(lax.all_gather(amplitudes, 'amp', axis=0, tiled=True), integrals,...]
    all_to_all x2 -> x0, local copies, waits for them, and re-layouts: 7.12 us -> none  [local(): lax.all_to_all(partial_value, 'amp', split_axis=0, concat_axis=1, tiled=T...]
    reshape x1 -> x0, local copies, waits for them, and re-layouts: 5.38 us -> none  [local(): partial_value = partial_value.reshape(rows_dev * amp_count, ABD, TILE)]
  transfers between devices with their start and end apart: 3 -> 0, of which waited for: 3 -> 0; matrix products, arithmetic and copies ran while one was open for 0% -> 0% of each run, Pallas kernels for 0% -> 0%
where the time goes in v1:
time: 85.2 us; the launch traced here: 85.1 us
  Pallas kernels  83.2 us (98%)
  other arithmetic  1.89 us (2%)
    pallas_call x1, Pallas kernels, local(): pl.pallas_call(kernel, name='ladder', out_shape=jax.ShapeDtypeStruct((64,...  83.2 us
    add x1, other arithmetic, local(): return residual_in + ladder  1.89 us

profile of v1, /device:TPU:32, one launch (start us, length us, event | category | flops | bytes accessed | tf_op | source)
XLA Modules:
  0.0 85.1 jit_solution(4246491955297346469)
XLA Ops:
  0.0 0.0 copy-start
  0.0 83.2 %ladder.1 = f32[64,2048]{1,0:T(8,128)} custom-call(bf16[64,2048]{1,0:T(8,128)(2,1)} %amp_ref.1, bf16[2048,1024]{1,0:T(8,128)(2,1)} %int_hbm.1, s32[16,128]{1,0:T(8,128)} %map_ref.1), custom_call_target="tpu_custom_call" | custom-call | tf_op jit(solution)/shard_map/ladder/pallas_call | solution.py:320
  83.2 0.0 copy-done
  83.2 1.9 %add.3 = f32[64,2048]{1,0:T(8,128)} add(f32[64,2048]{1,0:T(8,128)S(1)} %copy-done, f32[64,2048]{1,0:T(8,128)} %ladder.1) | non-fusion elementwise | flops 131072 | bytes 1572864 | tf_op jit(solution)/shard_map/add | solution.py:346
Async XLA Ops:
  0.0 83.2 %copy-start = (f32[64,2048]{1,0:T(8,128)S(1)}, f32[64,2048]{1,0:T(8,128)}, u32[]{:S(2)}) copy-start(f32[64,2048]{1,0:T(8,128)} %param.7) | copy-start | bytes 1572868

commit v2 on v1

--- a/solution.py
+++ b/solution.py
@@ -11,7 +11,7 @@
 F32, BF16, I16 = jnp.float32, jnp.bfloat16, jnp.int16
 
 TOP = math.log2(1537.0)
-SPAN = 24.0
+SPAN = 28.0
 STEPS = 32700.0 / SPAN
 LOW = TOP - SPAN
 XMIN = 2.0 ** LOW
@@ -42,7 +42,7 @@
 
 
 def kernel(amp_ref, int_hbm, map_ref, out_ref,
-           g, b, f, e, r13, r04, d, sb, rb, fs, fr, pick,
+           g, b, f, e13, e04, r13, r04, d, sb, rb, fs, fr, pick,
            ag_send, ag_recv, sib_send, sib_recv, loc_sem,
            xa_send, xa_recv, xa_loc, rs_send, rs_recv, fin_send, fin_recv, fin_loc):
     i = lax.axis_index("ints")
@@ -59,11 +59,6 @@
         j = lax.rem(x + dj // 4, 4) * 4 + lax.rem(y + lax.rem(dj, 4), 4)
         return j, lax.rem(c + lax.rem(t, 2), 2)
 
-    load_b = pltpu.make_async_copy(int_hbm, b, loc_sem.at[0])
-    load_b.start()
-    own = pltpu.make_async_copy(amp_ref, g.at[0, pl.ds(lane0, 64)], loc_sem.at[1])
-    own.start()
-
     barrier = pltpu.get_barrier_semaphore()
 
     def greet(t, carry):
@@ -74,6 +69,43 @@
         for cc in (0, 1):
             pl.semaphore_signal(barrier, inc=1, device_id=(i, zn * 2 + cc), device_id_type=MESH)
     lax.fori_loop(1, 32, greet, 0)
+
+    load_b = pltpu.make_async_copy(int_hbm, b, loc_sem.at[0])
+    load_b.start()
+    own = pltpu.make_async_copy(amp_ref, g.at[0, pl.ds(lane0, 64)], loc_sem.at[1])
+    own.start()
+    pl.semaphore_wait(barrier, 35)
+
+    def part(ref, p):
+        return ref.at[pl.ds(pl.multiple_of(lane0 + p * 32, 32), 32)]
+
+    def slot(direction, k):
+        return 0 if k == 0 else 7 if k == 4 else 2 * k - 1 + direction
+
+    def hop(direction, k, p):
+        src = amp_ref.at[pl.ds(p * 32, 32)] if k == 1 else part(g.at[slot(direction, k - 1)], p)
+        return pltpu.make_async_remote_copy(
+            src_ref=src, dst_ref=part(g.at[slot(direction, k)], p),
+            send_sem=ag_send.at[direction, k - 1, p], recv_sem=ag_recv.at[direction, k - 1, p],
+            device_id=(right, left)[direction], device_id_type=MESH)
+
+    def share(direction, k, p):
+        ref = part(g.at[slot(direction, k)], p)
+        return pltpu.make_async_remote_copy(
+            src_ref=ref, dst_ref=ref,
+            send_sem=sib_send.at[direction, k - 1, p], recv_sem=sib_recv.at[direction, k - 1, p],
+            device_id=sib, device_id_type=MESH)
+
+    def pieces(direction, k):
+        return (0, 1) if k < 4 else (direction,)
+
+    for p in (0, 1):
+        for direction in (0, 1):
+            hop(direction, 1, p).start()
+    share0 = pltpu.make_async_remote_copy(
+        src_ref=amp_ref, dst_ref=g.at[0, pl.ds(lane0, 64)], send_sem=loc_sem.at[2], recv_sem=loc_sem.at[3],
+        device_id=sib, device_id_type=MESH)
+    share0.start()
 
     lane = lax.broadcasted_iota(jnp.int32, (128, 256), 0)
     ent = lax.broadcasted_iota(jnp.int32, (128, 256), 1)
@@ -85,39 +117,6 @@
     tiles = lax.broadcasted_iota(jnp.int32, (256, 256), 0).astype(F32)
     pick[...] = jnp.where(tiles == ids, 1.0, 0.0).astype(BF16)
 
-    pl.semaphore_wait(barrier, 35)
-
-    def part(ref, p):
-        return ref.at[pl.ds(pl.multiple_of(lane0 + p * 32, 32), 32)]
-
-    def slot(direction, k):
-        return 0 if k == 0 else 7 if k == 4 else 2 * k - 1 + direction
-
-    def hop(direction, k, p):
-        src = amp_ref.at[pl.ds(p * 32, 32)] if k == 1 else part(g.at[slot(direction, k - 1)], p)
-        return pltpu.make_async_remote_copy(
-            src_ref=src, dst_ref=part(g.at[slot(direction, k)], p),
-            send_sem=ag_send.at[direction, k - 1, p], recv_sem=ag_recv.at[direction, k - 1, p],
-            device_id=(right, left)[direction], device_id_type=MESH)
-
-    def share(direction, k, p):
-        ref = part(g.at[slot(direction, k)], p)
-        return pltpu.make_async_remote_copy(
-            src_ref=ref, dst_ref=ref,
-            send_sem=sib_send.at[direction, k - 1, p], recv_sem=sib_recv.at[direction, k - 1, p],
-            device_id=sib, device_id_type=MESH)
-
-    def pieces(direction, k):
-        return (0, 1) if k < 4 else (direction,)
-
-    for p in (0, 1):
-        for direction in (0, 1):
-            hop(direction, 1, p).start()
-    share0 = pltpu.make_async_remote_copy(
-        src_ref=amp_ref, dst_ref=g.at[0, pl.ds(lane0, 64)], send_sem=loc_sem.at[2], recv_sem=loc_sem.at[3],
-        device_id=sib, device_id_type=MESH)
-    share0.start()
-
     def pass_on(k):
         for p in (0, 1):
             for direction in (0, 1):
@@ -126,7 +125,9 @@
                     if k < 4 and p in pieces(direction, k + 1):
                         hop(direction, k + 1, p).start()
                     share(direction, k, p).start()
-        for p in (0, 1):
+
+    def shared(k, halves=(0, 1)):
+        for p in halves:
             for direction in (0, 1):
                 if p in pieces(direction, k):
                     share(direction, k, p).wait_recv()
@@ -147,14 +148,63 @@
             base = pl.multiple_of(q * 256, 256)
             even = f[pl.ds(base, 128), :].reshape(16, 8, 128)
             odd = f[pl.ds(base + 128, 128), :].reshape(16, 8, 128)
-            e[first + q // 4, lax.rem(q // 2, 2), lax.rem(q, 2)] = jnp.concatenate([even, odd], axis=1).astype(I16)
+            codes = jnp.concatenate([even, odd], axis=1).astype(I16)
+            blk_at, row_lane, rp = q // 4, lax.rem(q // 2, 2), lax.rem(q, 2)
+            if count == 2:
+                e13[first // 2, 1 - blk_at, :, row_lane, rp] = codes
+            else:
+                e04[first // 7, row_lane, :, rp] = codes
             return carry
         lax.fori_loop(0, 4 * count, pack, 0)
+
+    def multiply3(p):
+        def columns(n, carry):
+            rows = jnp.concatenate([
+                g[s, lane * 64 + p * 32:lane * 64 + p * 32 + 32] for s in (5, 6) for lane in (0, 1)], axis=0)
+            acc = jnp.dot(rows, b[:, pl.ds(pl.multiple_of(n * 256, 256), 256)], preferred_element_type=F32)
+            code = log_code(acc)
+            for s in (0, 1):
+                f[pl.ds(2 * n + s, 128, stride=8), :] = code[:, s * 128:(s + 1) * 128]
+            return carry
+        lax.fori_loop(0, 4, columns, 0)
+        for q in range(4):
+            even = f[q * 256:q * 256 + 128, :].reshape(16, 8, 128)
+            odd = f[q * 256 + 128:q * 256 + 256, :].reshape(16, 8, 128)
+            e13[2, 1 - q // 2, :, q % 2, p] = jnp.concatenate([even, odd], axis=1).astype(I16)
+
+    def deal3(p):
+        at = 3 if p == 0 else 5
+
+        def refs(j, cc):
+            return e13.at[2, cc, j, :, p], r13.at[2, me, :, p]
+        src, dst = refs(i, c)
+        pltpu.make_async_copy(src, dst, xa_loc.at[at]).start()
+
+        def one(t, carry):
+            j, cc = peer(t)
+            src, dst = refs(j, cc)
+            pltpu.make_async_remote_copy(
+                src_ref=src, dst_ref=dst, send_sem=xa_send.at[at], recv_sem=xa_recv.at[at],
+                device_id=(j, zz * 2 + cc), device_id_type=MESH).start()
+            return carry
+        lax.fori_loop(1, 32, one, 0)
+
+    def deal3_all(p):
+        at = 3 if p == 0 else 5
+        ref = r13.at[2, pl.ds(0, 31), :, p]
+        return pltpu.make_async_remote_copy(
+            src_ref=ref, dst_ref=ref, send_sem=xa_send.at[at], recv_sem=xa_recv.at[at],
+            device_id=sib, device_id_type=MESH)
+
+    def gathered3(p):
+        at = 3 if p == 0 else 5
+        pltpu.make_async_copy(e13.at[2, c, i, :, p], r13.at[2, me, :, p], xa_loc.at[at]).wait()
+        deal3_all(p).wait_recv()
 
     def deal_refs(k, j, cc):
         if k in (0, 4):
-            return e.at[0 if k == 0 else 7, cc, :, j], r04.at[k // 4, me]
-        return e.at[2 * k - cc, :, :, j], r13.at[k - 1, me]
+            return e04.at[k // 4, cc, j], r04.at[k // 4, me]
+        return e13.at[k - 1, cc, j], r13.at[k - 1, me]
 
     def deal(k):
         def one(t, carry):
@@ -235,20 +285,30 @@
     load_b.wait()
     multiply(0, 1)
     deal(0)
-    for k in (1, 2, 3):
-        pass_on(k)
+    pass_on(1)
+    for k in (1, 2):
+        shared(k)
         multiply(2 * k - 1, 2)
+        pass_on(k + 1)
         deal(k)
         dense(k - 1)
+    shared(3, (0,))
+    multiply3(0)
+    deal3(0)
+    shared(3, (1,))
+    multiply3(1)
     pass_on(4)
+    deal3(1)
+    shared(4)
     multiply(7, 1)
     deal(4)
-    dense(3)
-
-    def rest3(p, carry):
+    for p in (0, 1):
+        gathered3(p)
+        add_up(r13[2, :, 1 - c, p], 8 + (1 - c) * 2 + p)
         send_chain(3, 1 - c, p)
-        return carry
-    lax.fori_loop(0, 2, rest3, 0)
+    for p in (0, 1):
+        add_up(r13[2, :, c, p], 8 + c * 2 + p)
+    dense(2)
     dense(4)
 
     def first4(p, carry):
@@ -256,31 +316,36 @@
         return carry
     lax.fori_loop(0, 2, first4, 0)
 
+    def run(k, lane):
+        def one(p, carry):
+            send_chain(k, lane, p)
+            return carry
+        lax.fori_loop(0, 2, one, 0)
+
     def own3(p, carry):
         send_chain3(p)
         return carry
+    run(2, 1 - c)
     lax.fori_loop(0, 2, own3, 0)
-    for k in (2, 1):
-        def step(q, carry):
-            lane = jnp.where(q < 2, 1 - c, c)
-            send_chain(k, lane, lax.rem(q, 2))
-            return carry
-        lax.fori_loop(0, 4, step, 0)
+    run(1, 1 - c)
+    run(2, c)
+    run(1, c)
+
+    mine = pl.ds(pl.multiple_of(i * 32, 32), 32)
 
     def last(p, j):
         return pltpu.make_async_remote_copy(
-            src_ref=fs.at[p, :, pl.ds(pl.multiple_of(j * 16, 16), 16)],
-            dst_ref=fr.at[p, :, pl.ds(pl.multiple_of(i * 16, 16), 16)],
+            src_ref=fs.at[p, j].reshape(32, 128),
+            dst_ref=fr.at[p, mine],
             send_sem=fin_send.at[p], recv_sem=fin_recv.at[p], device_id=(j, zz * 2 + c), device_id_type=MESH)
 
     def keep(p):
-        mine = pl.ds(pl.multiple_of(i * 16, 16), 16)
-        return pltpu.make_async_copy(fs.at[p, :, mine], fr.at[p, :, mine], fin_loc.at[p])
+        return pltpu.make_async_copy(fs.at[p, i].reshape(32, 128), fr.at[p, mine], fin_loc.at[p])
 
     for p in (0, 1):
         total = d[12 + p] + arrived(10 + p) + arrived(12 + p)
-        fs[p, 0] = total[:, 0:128]
-        fs[p, 1] = total[:, 128:256]
+        fs[p, :, 0] = total[:, 0:128].reshape(16, 16, 128)
+        fs[p, :, 1] = total[:, 128:256].reshape(16, 16, 128)
         keep(p).start()
 
         def owners(t, carry):
@@ -290,7 +355,7 @@
         lax.fori_loop(1, 16, owners, 0)
     for p in (0, 1):
         keep(p).wait()
-        every = fr.at[p, :, pl.ds(0, 240)]
+        every = fr.at[p, pl.ds(0, 480)]
         done = pltpu.make_async_remote_copy(
             src_ref=every, dst_ref=every, send_sem=fin_send.at[p], recv_sem=fin_recv.at[p],
             device_id=sib, device_id_type=MESH)
@@ -298,7 +363,7 @@
         for rr in (0, 1):
             for t in range(16):
                 out_ref[p * 32 + rr * 16:p * 32 + rr * 16 + 16, t * 128:(t + 1) * 128] = (
-                    fr[p, rr, pl.ds(t, 16, stride=16), :])
+                    fr[p, pl.ds(rr * 16 + t, 16, stride=32), :])
         done.wait_send()
 
     share0.wait_send()
@@ -307,8 +372,10 @@
             for p in pieces(direction, k):
                 hop(direction, k, p).wait_send()
                 share(direction, k, p).wait_send()
-    for k in range(5):
+    for k in (0, 1, 2, 4):
         deal_all(k).wait_send()
+    deal3_all(0).wait_send()
+    deal3_all(1).wait_send()
     for m in range(14):
         pltpu.make_async_remote_copy(
             src_ref=sb.at[m], dst_ref=rb.at[m], send_sem=rs_send.at[m], recv_sem=rs_recv.at[m],
@@ -321,27 +388,28 @@
         kernel,
         name="ladder",
         out_shape=jax.ShapeDtypeStruct((64, 2048), F32),
-        in_specs=[pl.BlockSpec(memory_space=pltpu.VMEM), pl.BlockSpec(memory_space=pl.ANY),
+        in_specs=[pl.BlockSpec(memory_space=pl.ANY), pl.BlockSpec(memory_space=pl.ANY),
                   pl.BlockSpec(memory_space=pltpu.VMEM)],
         out_specs=pl.BlockSpec(memory_space=pltpu.VMEM),
         scratch_shapes=[
             pltpu.VMEM((8, 128, 2048), BF16),
             pltpu.VMEM((2048, 1024), BF16),
             pltpu.VMEM((2048, 128), F32),
-            pltpu.VMEM((8, 2, 2, 16, 16, 128), I16),
+            pltpu.VMEM((3, 2, 16, 2, 2, 16, 128), I16),
+            pltpu.VMEM((2, 2, 16, 2, 16, 128), I16),
             pltpu.VMEM((3, 32, 2, 2, 16, 128), I16),
             pltpu.VMEM((2, 32, 2, 16, 128), I16),
             pltpu.VMEM((16, 256, 256), F32),
             pltpu.VMEM((14, 272, 256), I16),
             pltpu.VMEM((14, 272, 256), I16),
-            pltpu.VMEM((2, 2, 256, 128), F32),
-            pltpu.VMEM((2, 2, 256, 128), F32),
+            pltpu.VMEM((2, 16, 2, 16, 128), F32),
+            pltpu.VMEM((2, 512, 128), F32),
             pltpu.VMEM((256, 256), BF16),
             dma((2, 4, 2)), dma((2, 4, 2)), dma((2, 4, 2)), dma((2, 4, 2)), dma((4,)),
-            dma((5,)), dma((5,)), dma((5,)), dma((14,)), dma((14,)), dma((2,)), dma((2,)), dma((2,)),
+            dma((6,)), dma((6,)), dma((6,)), dma((14,)), dma((14,)), dma((2,)), dma((2,)), dma((2,)),
         ],
         compiler_params=pltpu.CompilerParams(
-            collective_id=0, has_side_effects=True, vmem_limit_bytes=56 * 2**20),
+            collective_id=0, has_side_effects=True, vmem_limit_bytes=50 * 2**20),
     )(amplitudes, integrals, tile_map)
     return residual_in + ladder
 

time: 85.2 us -> 80.9 us (0.950)
  Pallas kernels: 83.2 us -> 78.2 us
  local copies, waits for them, and re-layouts: 0.01 us -> 1.65 us
  other arithmetic: 1.89 us -> 0.85 us
    pallas_call x1, Pallas kernels: 83.2 us -> 78.2 us  [local(): pl.pallas_call(kernel, name='ladder', out_shape=jax.ShapeDtypeStruct((64,...]
    unnamed x2 -> x6, local copies, waits for them, and re-layouts: 0.01 us -> 1.65 us
    add x1, other arithmetic: 1.89 us -> 0.85 us  [local(): return residual_in + ladder]
where the time goes in v2:
time: 80.9 us; the launch traced here: 80.7 us
  Pallas kernels  78.2 us (97%)
  local copies, waits for them, and re-layouts  1.65 us (2%)
  other arithmetic  0.85 us (1%)
    pallas_call x1, Pallas kernels, local(): pl.pallas_call(kernel, name='ladder', out_shape=jax.ShapeDtypeStruct((64,...  78.2 us
    unnamed x6, local copies, waits for them, and re-layouts  1.65 us

profile of v2, /device:TPU:32, one launch (start us, length us, event | category | flops | bytes accessed | tf_op | source)
XLA Modules:
  0.0 80.7 jit_solution(9347866752131112181)
XLA Ops:
  0.0 0.0 copy-start
  0.0 0.9 %copy-done = bf16[64,2048]{1,0:T(8,128)(2,1)S(1)} copy-done((bf16[64,2048]{1,0:T(8,128)(2,1)S(1)}, bf16[64,2048]{1,0:T(8,128)(2,1)}, u32[]{:S(2)}) %copy-start) | copy-done | bytes 262168
  1.0 0.0 copy-start.1
  1.0 0.7 copy-done.1
  1.6 0.0 copy-start.2
  1.7 78.2 %ladder.1 = f32[64,2048]{1,0:T(8,128)S(1)} custom-call(bf16[64,2048]{1,0:T(8,128)(2,1)S(1)} %copy-done, bf16[2048,1024]{1,0:T(8,128)(2,1)} %int_hbm.1, s32[16,128]{1,0:T(8,128)S(1)} %copy-done.1), custom_call_target="tpu_custom_call" | custom-call | tf_op jit(solution)/shard_map/ladder/pallas_call | solution.py:387
  79.8 0.0 copy-done.2
  79.9 0.9 %add.3 = f32[64,2048]{1,0:T(8,128)} add(f32[64,2048]{1,0:T(8,128)S(1)} %copy-done.2, f32[64,2048]{1,0:T(8,128)S(1)} %ladder.1) | non-fusion elementwise | flops 131072 | bytes 1572864 | tf_op jit(solution)/shard_map/add | solution.py:414
Async XLA Ops:
  0.0 0.9 %copy-start = (bf16[64,2048]{1,0:T(8,128)(2,1)S(1)}, bf16[64,2048]{1,0:T(8,128)(2,1)}, u32[]{:S(2)}) copy-start(bf16[64,2048]{1,0:T(8,128)(2,1)} %amp_ref.1) | copy-start | bytes 786436
  1.0 0.7 copy-start.1
  1.6 78.2 %copy-start.2 = (f32[64,2048]{1,0:T(8,128)S(1)}, f32[64,2048]{1,0:T(8,128)}, u32[]{:S(2)}) copy-start(f32[64,2048]{1,0:T(8,128)} %param.7) | copy-start | bytes 1572868

commit v3 on v2

--- a/solution.py
+++ b/solution.py
@@ -33,12 +33,29 @@
     power = jnp.ceil(jnp.log2(jnp.maximum(top, 1e-30)) * 64.0)
     q = x * (jnp.exp2(power * (-1.0 / 64.0)) * 32700.0)[None]
     q = jnp.where(q < 0, q - 0.5, q + 0.5)
-    return q.reshape(256, 256).astype(I16), jnp.concatenate([power, power], axis=0).astype(I16)
-
-
-def chain_value(codes, powers):
-    scale = jnp.exp2(powers.astype(F32)[0:8] * (1.0 / 64.0)) * (1.0 / 32700.0)
-    return (codes.astype(F32).reshape(32, 8, 256) * scale[None]).reshape(256, 256)
+    q = q.reshape(256, 256).astype(I16)
+    power = jnp.concatenate([power[:, 0:128], power[:, 128:256]], axis=0).astype(I16)
+    return q[:, 0:128], q[:, 128:256], power
+
+
+def chain_value(first, second, powers):
+    scale = jnp.exp2(powers.astype(F32) * (1.0 / 64.0)) * (1.0 / 32700.0)
+    first = first.astype(F32).reshape(32, 8, 128) * scale[None, 0:8]
+    second = second.astype(F32).reshape(32, 8, 128) * scale[None, 8:16]
+    return jnp.concatenate([first.reshape(256, 128), second.reshape(256, 128)], axis=1)
+
+
+def final_code(total):
+    x = total.reshape(16, 16, 256)
+    top = jnp.max(jnp.abs(x), axis=1, keepdims=True)
+    top = jnp.maximum(top[:, :, 0:128], top[:, :, 128:256])
+    power = jnp.ceil(jnp.log2(jnp.maximum(top, 1e-30)) * 64.0)
+    scale = jnp.exp2(power * (-1.0 / 64.0)) * 32700.0
+
+    def whole(q):
+        return jnp.where(q < 0, q - 0.5, q + 0.5).astype(I16)
+    return (whole(x[:, :, 0:128] * scale), whole(x[:, :, 128:256] * scale),
+            jnp.broadcast_to(power, (16, 16, 128)).astype(I16))
 
 
 def kernel(amp_ref, int_hbm, map_ref, out_ref,
@@ -263,7 +280,7 @@
         pltpu.make_async_remote_copy(
             src_ref=rb.at[m], dst_ref=rb.at[m], send_sem=rs_send.at[m], recv_sem=rs_recv.at[m],
             device_id=sib, device_id_type=MESH).wait_recv()
-        return chain_value(rb[m, 0:256], rb[m, 256:272])
+        return chain_value(rb[m, 0:256], rb[m, 256:512], rb[m, 512:528])
 
     def send_chain(k, lane, p):
         own_at = 14 + p if k == 4 else (k - 1) * 4 + lane * 2 + p
@@ -271,13 +288,13 @@
         if k < 3:
             value = value + arrived((6, 2)[k - 1] + lane * 2 + p)
         m, copy = chain(k, lane, p)
-        sb[m, 0:256], sb[m, 256:272] = chain_code(value)
+        sb[m, 0:256], sb[m, 256:512], sb[m, 512:528] = chain_code(value)
         copy.start()
 
     def send_chain3(p):
         value = d[8 + c * 2 + p] + arrived(p)
         m, copy = chain(3, c, p)
-        sb[m, 0:256], sb[m, 256:272] = chain_code(value)
+        sb[m, 0:256], sb[m, 256:512], sb[m, 512:528] = chain_code(value)
         copy.start()
 
     own.wait()
@@ -291,7 +308,8 @@
         multiply(2 * k - 1, 2)
         pass_on(k + 1)
         deal(k)
-        dense(k - 1)
+        if k == 1:
+            dense(0)
     shared(3, (0,))
     multiply3(0)
     deal3(0)
@@ -308,7 +326,6 @@
         send_chain(3, 1 - c, p)
     for p in (0, 1):
         add_up(r13[2, :, c, p], 8 + c * 2 + p)
-    dense(2)
     dense(4)
 
     def first4(p, carry):
@@ -325,27 +342,26 @@
     def own3(p, carry):
         send_chain3(p)
         return carry
+    dense(2)
+    dense(1)
     run(2, 1 - c)
     lax.fori_loop(0, 2, own3, 0)
     run(1, 1 - c)
     run(2, c)
     run(1, c)
 
-    mine = pl.ds(pl.multiple_of(i * 32, 32), 32)
-
     def last(p, j):
         return pltpu.make_async_remote_copy(
-            src_ref=fs.at[p, j].reshape(32, 128),
-            dst_ref=fr.at[p, mine],
+            src_ref=fs.at[p, j],
+            dst_ref=fr.at[p, i],
             send_sem=fin_send.at[p], recv_sem=fin_recv.at[p], device_id=(j, zz * 2 + c), device_id_type=MESH)
 
     def keep(p):
-        return pltpu.make_async_copy(fs.at[p, i].reshape(32, 128), fr.at[p, mine], fin_loc.at[p])
+        return pltpu.make_async_copy(fs.at[p, i], fr.at[p, i], fin_loc.at[p])
 
     for p in (0, 1):
         total = d[12 + p] + arrived(10 + p) + arrived(12 + p)
-        fs[p, :, 0] = total[:, 0:128].reshape(16, 16, 128)
-        fs[p, :, 1] = total[:, 128:256].reshape(16, 16, 128)
+        fs[p, :, 0:16], fs[p, :, 16:32], fs[p, :, 32:48] = final_code(total)
         keep(p).start()
 
         def owners(t, carry):
@@ -355,15 +371,18 @@
         lax.fori_loop(1, 16, owners, 0)
     for p in (0, 1):
         keep(p).wait()
-        every = fr.at[p, pl.ds(0, 480)]
+        every = fr.at[p, pl.ds(0, 15)]
         done = pltpu.make_async_remote_copy(
             src_ref=every, dst_ref=every, send_sem=fin_send.at[p], recv_sem=fin_recv.at[p],
             device_id=sib, device_id_type=MESH)
         done.wait_recv()
+        scale = jnp.exp2(fr[p, :, 32:48].astype(F32) * (1.0 / 64.0)) * (1.0 / 32700.0)
         for rr in (0, 1):
+            f[p * 512 + rr * 256:p * 512 + rr * 256 + 256, :] = (
+                fr[p, :, rr * 16:rr * 16 + 16].astype(F32) * scale).reshape(256, 128)
             for t in range(16):
                 out_ref[p * 32 + rr * 16:p * 32 + rr * 16 + 16, t * 128:(t + 1) * 128] = (
-                    fr[p, pl.ds(rr * 16 + t, 16, stride=32), :])
+                    f[pl.ds(p * 512 + rr * 256 + t, 16, stride=16), :])
         done.wait_send()
 
     share0.wait_send()
@@ -400,10 +419,10 @@
             pltpu.VMEM((3, 32, 2, 2, 16, 128), I16),
             pltpu.VMEM((2, 32, 2, 16, 128), I16),
             pltpu.VMEM((16, 256, 256), F32),
-            pltpu.VMEM((14, 272, 256), I16),
-            pltpu.VMEM((14, 272, 256), I16),
-            pltpu.VMEM((2, 16, 2, 16, 128), F32),
-            pltpu.VMEM((2, 512, 128), F32),
+            pltpu.VMEM((14, 528, 128), I16),
+            pltpu.VMEM((14, 528, 128), I16),
+            pltpu.VMEM((2, 16, 48, 128), I16),
+            pltpu.VMEM((2, 16, 48, 128), I16),
             pltpu.VMEM((256, 256), BF16),
             dma((2, 4, 2)), dma((2, 4, 2)), dma((2, 4, 2)), dma((2, 4, 2)), dma((4,)),
             dma((6,)), dma((6,)), dma((6,)), dma((14,)), dma((14,)), dma((2,)), dma((2,)), dma((2,)),

time: 80.9 us -> 79.9 us (0.988)
  Pallas kernels: 78.2 us -> 77.2 us
    pallas_call x1, Pallas kernels: 78.2 us -> 77.2 us  [local(): pl.pallas_call(kernel, name='ladder', out_shape=jax.ShapeDtypeStruct((64,...]
where the time goes in v3:
time: 79.9 us; the launch traced here: 79.7 us
  Pallas kernels  77.2 us (97%)
  local copies, waits for them, and re-layouts  1.65 us (2%)
  other arithmetic  0.85 us (1%)
    pallas_call x1, Pallas kernels, local(): pl.pallas_call(kernel, name='ladder', out_shape=jax.ShapeDtypeStruct((64,...  77.2 us
    unnamed x6, local copies, waits for them, and re-layouts  1.65 us

profile of v3, /device:TPU:32, one launch (start us, length us, event | category | flops | bytes accessed | tf_op | source)
XLA Modules:
  0.0 79.7 jit_solution(523905783382016283)
XLA Ops:
  0.0 0.0 copy-start
  0.0 0.9 %copy-done = bf16[64,2048]{1,0:T(8,128)(2,1)S(1)} copy-done((bf16[64,2048]{1,0:T(8,128)(2,1)S(1)}, bf16[64,2048]{1,0:T(8,128)(2,1)}, u32[]{:S(2)}) %copy-start) | copy-done | bytes 262168
  1.0 0.0 copy-start.1
  1.0 0.7 copy-done.1
  1.6 0.0 copy-start.2
  1.7 77.2 %ladder.1 = f32[64,2048]{1,0:T(8,128)S(1)} custom-call(bf16[64,2048]{1,0:T(8,128)(2,1)S(1)} %copy-done, bf16[2048,1024]{1,0:T(8,128)(2,1)} %int_hbm.1, s32[16,128]{1,0:T(8,128)S(1)} %copy-done.1), custom_call_target="tpu_custom_call" | custom-call | tf_op jit(solution)/shard_map/ladder/pallas_call | solution.py:406
  78.9 0.0 copy-done.2
  78.9 0.9 %add.3 = f32[64,2048]{1,0:T(8,128)} add(f32[64,2048]{1,0:T(8,128)S(1)} %copy-done.2, f32[64,2048]{1,0:T(8,128)S(1)} %ladder.1) | non-fusion elementwise | flops 131072 | bytes 1572864 | tf_op jit(solution)/shard_map/add | solution.py:433
Async XLA Ops:
  0.0 0.9 %copy-start = (bf16[64,2048]{1,0:T(8,128)(2,1)S(1)}, bf16[64,2048]{1,0:T(8,128)(2,1)}, u32[]{:S(2)}) copy-start(bf16[64,2048]{1,0:T(8,128)(2,1)} %amp_ref.1) | copy-start | bytes 786436
  1.0 0.7 copy-start.1
  1.6 77.2 %copy-start.2 = (f32[64,2048]{1,0:T(8,128)S(1)}, f32[64,2048]{1,0:T(8,128)}, u32[]{:S(2)}) copy-start(f32[64,2048]{1,0:T(8,128)} %param.7) | copy-start | bytes 1572868

commit v4 on v3

--- a/solution.py
+++ b/solution.py
@@ -331,7 +331,9 @@
     def first4(p, carry):
         send_chain(4, c, p)
         return carry
-    lax.fori_loop(0, 2, first4, 0)
+    first4(0, 0)
+    dense(2)
+    first4(1, 0)
 
     def run(k, lane):
         def one(p, carry):
@@ -342,7 +344,6 @@
     def own3(p, carry):
         send_chain3(p)
         return carry
-    dense(2)
     dense(1)
     run(2, 1 - c)
     lax.fori_loop(0, 2, own3, 0)

time: 79.9 us -> 79.9 us (level)
  no operation moved by 1% of the time
where the time goes in v4:
time: 79.9 us; the launch traced here: 79.7 us
  Pallas kernels  77.2 us (97%)
  local copies, waits for them, and re-layouts  1.65 us (2%)
  other arithmetic  0.85 us (1%)
    pallas_call x1, Pallas kernels, local(): pl.pallas_call(kernel, name='ladder', out_shape=jax.ShapeDtypeStruct((64,...  77.2 us
    unnamed x6, local copies, waits for them, and re-layouts  1.65 us

profile of v4, /device:TPU:32, one launch (start us, length us, event | category | flops | bytes accessed | tf_op | source)
XLA Modules:
  0.0 79.7 jit_solution(14706261701298062053)
XLA Ops:
  0.0 0.0 copy-start
  0.0 0.9 %copy-done = bf16[64,2048]{1,0:T(8,128)(2,1)S(1)} copy-done((bf16[64,2048]{1,0:T(8,128)(2,1)S(1)}, bf16[64,2048]{1,0:T(8,128)(2,1)}, u32[]{:S(2)}) %copy-start) | copy-done | bytes 262168
  1.0 0.0 copy-start.1
  1.0 0.7 copy-done.1
  1.6 0.0 copy-start.2
  1.7 77.2 %ladder.1 = f32[64,2048]{1,0:T(8,128)S(1)} custom-call(bf16[64,2048]{1,0:T(8,128)(2,1)S(1)} %copy-done, bf16[2048,1024]{1,0:T(8,128)(2,1)} %int_hbm.1, s32[16,128]{1,0:T(8,128)S(1)} %copy-done.1), custom_call_target="tpu_custom_call" | custom-call | tf_op jit(solution)/shard_map/ladder/pallas_call | solution.py:407
  78.9 0.0 copy-done.2
  78.9 0.9 %add.3 = f32[64,2048]{1,0:T(8,128)} add(f32[64,2048]{1,0:T(8,128)S(1)} %copy-done.2, f32[64,2048]{1,0:T(8,128)S(1)} %ladder.1) | non-fusion elementwise | flops 131072 | bytes 1572864 | tf_op jit(solution)/shard_map/add | solution.py:434
Async XLA Ops:
  0.0 0.9 %copy-start = (bf16[64,2048]{1,0:T(8,128)(2,1)S(1)}, bf16[64,2048]{1,0:T(8,128)(2,1)}, u32[]{:S(2)}) copy-start(bf16[64,2048]{1,0:T(8,128)(2,1)} %amp_ref.1) | copy-start | bytes 786436
  1.0 0.7 copy-start.1
  1.6 77.2 %copy-start.2 = (f32[64,2048]{1,0:T(8,128)S(1)}, f32[64,2048]{1,0:T(8,128)}, u32[]{:S(2)}) copy-start(f32[64,2048]{1,0:T(8,128)} %param.7) | copy-start | bytes 1572868
